TPU v7x, 128 devices: a whole 4x4x4 slice. The times are simulated.
128 devices in a mesh: hst: 16 (over z, x), doc: 8 (over y, core).
Axes of the slice: x: 4, y: 4, z: 4, core: 2. Of those that a mesh axis runs over, the one named last changes fastest.
Arguments:
- docs: bfloat16 [1048576, 768], P(('hst', 'doc')), may hold values from -400 to 400, as said below
- w_in: bfloat16 [768, 256], replicated, may hold values from -0.21875 to 0.21875
- w_out: bfloat16 [256, 64], replicated, may hold values from -0.375 to 0.375
- doc_host: int32 [1048576], P(('hst', 'doc')), may hold values from 0 to 2047
- tiles: bfloat16 [8192, 128, 128], P(('hst', 'doc')), may hold values from 0 to 10, as said below
- dst_block: int32 [8192], P(('hst', 'doc')), may hold values from 0 to 15
- src_block: int32 [8192], P(('hst', 'doc')), may hold values from 0 to 255
- tile_count: int32 [128], P(('hst', 'doc')), may hold values from 1 to 64, as said below
- teleport: int32 [32768], P('hst'), may hold values 0 or 1
Outputs:
- scores: float32 [32768, 64], P(('hst', 'doc'))
Inputs may be any that keep to these rules, and one draw needn't show every extreme that they name: `docs`: embeddings stay in the stated range. `tiles`: link weights are nonnegative. `tile_count`: some device uses all 64 slots.
All inputs are finite; a program needn't handle non-finite values. No bound on the sum of `teleport` on one device may be relied on, other than what follows from the above.
Results may differ from a plain program's by a relative error of at most 0.00066.
Values may be sent and summed in bfloat16 or wider, within the bound.
A program may use at most 128 MiB of HBM per device.

v0:
```python
import jax
import jax.numpy as jnp
from jax import lax
from jax.sharding import PartitionSpec as P

HOPS = 3


def body(docs, w_in, w_out, doc_host, tiles, dst_block, src_block, tile_count, teleport):
    host_dev = teleport.shape[0]
    block = tiles.shape[1]
    topics = w_out.shape[1]
    slots = tiles.shape[0]
    hosts_all = host_dev * lax.axis_size("hst")
    nblocks = hosts_all // block
    hidden = jax.nn.gelu(
        jnp.dot(docs, w_in, preferred_element_type=jnp.float32), approximate=True
    ).astype(jnp.bfloat16)
    probs = jax.nn.softmax(jnp.dot(hidden, w_out, preferred_element_type=jnp.float32), axis=-1)
    local_topic = jax.ops.segment_sum(probs, doc_host, num_segments=host_dev)
    used = (jnp.arange(slots) < tile_count[0]).astype(jnp.float32)
    colsum = jnp.sum(tiles, axis=1, dtype=jnp.float32)
    src_onehot = (src_block[:, None] == jnp.arange(nblocks)[None, :]).astype(jnp.float32) * used[
        :, None
    ]
    degree_blocks = jnp.dot(src_onehot.T, colsum, precision=lax.Precision.HIGHEST)
    degree = lax.psum(degree_blocks, ("hst", "doc")).reshape(hosts_all)
    own_degree = lax.dynamic_slice_in_dim(degree, lax.axis_index("hst") * host_dev, host_dev)
    inverse = 1.0 / jnp.maximum(own_degree, 1.0)
    dst_onehot = (dst_block[:, None] == jnp.arange(host_dev // block)[None, :]).astype(
        jnp.float32
    ) * used[:, None]
    member = teleport.astype(jnp.float32)
    rows = host_dev // lax.axis_size("doc")
    host_topic = lax.psum(local_topic, "doc")
    mass = lax.psum(jnp.sum(member[:, None] * host_topic, axis=0), "hst")
    tele = member[:, None] * host_topic / mass
    state = tele
    for hop in range(HOPS):
        sent = (state * inverse[:, None]).astype(jnp.bfloat16)
        full = lax.all_gather(sent, "hst", axis=0, tiled=True)
        slabs = full.reshape(nblocks, block, topics)[src_block]
        prod = jnp.einsum("kij,kjt->kit", tiles, slabs, preferred_element_type=jnp.float32)
        gathered = jnp.einsum("kb,kit->bit", dst_onehot, prod, precision=lax.Precision.HIGHEST)
        inflow = lax.psum(gathered.reshape(host_dev, topics), "doc")
        state = 0.85 * inflow + 0.15 * tele
    result = lax.dynamic_slice_in_dim(state, lax.axis_index("doc") * rows, rows)
    return hosts_all * result


def solution(mesh):
    placed = (
        P(("hst", "doc"), None),
        P(),
        P(),
        P(("hst", "doc")),
        P(("hst", "doc"), None, None),
        P(("hst", "doc")),
        P(("hst", "doc")),
        P(("hst", "doc")),
        P("hst"),
    )
    return jax.shard_map(
        body, mesh=mesh, in_specs=placed, out_specs=P(("hst", "doc"), None), check_vma=False
    )
```

profile of v0, /device:TPU:0, one launch (start us, length us, event | category | flops | bytes accessed | tf_op | source)
XLA Modules:
  0.0 640.4 jit_solution(17008999515403632906)
XLA Ops:
  7.3 2.1 convert_reduce_fusion
  9.4 1.8 convolution_bitcast_fusion
  11.2 8.6 %fusion.48 = (f32[8192]{0:T(1024)S(1)}, f32[8192,64]{0,1:T(8,128)S(1)}) fusion(bf16[256,64]{0,1:T(8,128)(2,1)} %param.11, bf16[8192,768]{1,0:T(8,128)(2,1)} %param.9, bf16[768,256]{1,0:T(8,128)(2,1)S(1)} %copy-done), kind=kOutput, calls=%fused_computation.78 | convolution fusion | flops 3509051392 | bytes 15138816 | tf_op jit(solution)/shard_map/dot_general | solution.py:19
  19.9 1.3 copy-done.2
  21.6 1.9 fusion.16
  23.5 2.7 copy.18
  26.2 44.5 %scatter_custom_fusion = f32[2048,64]{1,0:T(8,128)S(1)} fusion(s32[8192]{0:T(1024)} %param.12, f32[8192,64]{1,0:T(8,128)} %copy.18, f32[]{:T(128)} %constant.16.clone.1), kind=kCustom, calls=%fused_computation.37 | custom fusion | flops 524288 | bytes 524800 | tf_op jit(solution)/shard_map/scatter-add | solution.py:20
  72.0 82.8 %all-reduce.8.cloned.1.call-done = f32[32768]{0:T(1024)} async-done(((f32[32768]{0:T(1024)}), f32[32768]{0:T(1024)}) %all-reduce.8.cloned.1.call-update) | async-done | bytes 131088 | tf_op jit(solution)/shard_map/psum | solution.py:27
  155.5 59.7 %all-reduce.6.cloned.1.call-done = f32[2048,64]{0,1:T(8,128)} async-done(((f32[2048,64]{0,1:T(8,128)}), f32[2048,64]{0,1:T(8,128)}) %all-reduce.6.cloned.1.call-update) | async-done | bytes 524304 | tf_op jit(solution)/shard_map/psum | solution.py:35
  216.4 40.5 %psum.43 = f32[64]{0:T(128)S(1)} all-reduce(f32[64]{0:T(128)S(1)} %multiply_reduce_fusion), channel_id=1, replica_groups=mesh['hst'=16,'doc'=8] {'hst'}, use_global_device_ids=true, to_apply=%region_5.0 | all-reduce | flops 64 | bytes 512 | tf_op jit(solution)/shard_map/psum | solution.py:36
  256.9 1.9 multiply_convert_fusion.2
  259.7 44.7 %all-gather.4.cloned.1.call-done = bf16[32768,64]{0,1:T(8,128)(2,1)} async-done(((bf16[2048,64]{0,1:T(8,128)(2,1)}), bf16[32768,64]{0,1:T(8,128)(2,1)}) %all-gather.4.cloned.1.call-update) | async-done | bytes 4194320 | tf_op jit(solution)/shard_map/all_gather | solution.py:41
  304.4 5.4 copy_bitcast_fusion.2
  309.8 3.2 gather_fusion
  313.0 1.5 convolution_bitcast_fusion.3
  314.6 2.2 fusion.14
  317.8 60.4 %all-reduce.10.cloned.1.call-done = f32[2048,64]{0,1:T(8,128)} async-done(((f32[2048,64]{0,1:T(8,128)}), f32[2048,64]{0,1:T(8,128)}) %all-reduce.10.cloned.1.call-update) | async-done | bytes 524304 | tf_op jit(solution)/shard_map/psum | solution.py:45
  378.3 2.2 multiply_convert_fusion.1
  380.6 51.0 %all-gather.6.cloned.1.call-done = bf16[32768,64]{0,1:T(8,128)(2,1)} async-done(((bf16[2048,64]{0,1:T(8,128)(2,1)}), bf16[32768,64]{0,1:T(8,128)(2,1)}) %all-gather.6.cloned.1.call-update) | async-done | bytes 4194320 | tf_op jit(solution)/shard_map/all_gather | solution.py:41
  431.6 5.4 copy_bitcast_fusion.1
  436.9 3.1 gather_fusion.1
  440.0 1.5 convolution_bitcast_fusion.2
  441.6 2.2 fusion.12
  444.8 60.4 %all-reduce.12.cloned.1.call-done = f32[2048,64]{0,1:T(8,128)} async-done(((f32[2048,64]{0,1:T(8,128)}), f32[2048,64]{0,1:T(8,128)}) %all-reduce.12.cloned.1.call-update) | async-done | bytes 524304 | tf_op jit(solution)/shard_map/psum | solution.py:45
  505.3 1.8 multiply_convert_fusion
  507.4 51.0 %all-gather.8.cloned.1.call-done = bf16[32768,64]{0,1:T(8,128)(2,1)} async-done(((bf16[2048,64]{0,1:T(8,128)(2,1)}), bf16[32768,64]{0,1:T(8,128)(2,1)}) %all-gather.8.cloned.1.call-update) | async-done | bytes 4194320 | tf_op jit(solution)/shard_map/all_gather | solution.py:41
  558.4 5.4 copy_bitcast_fusion
  563.7 3.1 gather_fusion.2
  566.8 1.5 convolution_bitcast_fusion.1
  568.3 2.2 fusion.10
  571.6 60.5 %all-reduce.14.cloned.1.call-done = f32[2048,64]{0,1:T(8,128)} async-done(((f32[2048,64]{0,1:T(8,128)}), f32[2048,64]{0,1:T(8,128)}) %all-reduce.14.cloned.1.call-update) | async-done | bytes 524304 | tf_op jit(solution)/shard_map/psum | solution.py:45
  632.0 1.5 fusion.20
  (54 shorter events, 7.7 us)
Async XLA Ops:
  6.5 4.7 copy-start
  6.5 148.3 %all-reduce.8.cloned.1.call-start = ((), (), s32[]{:S(2)}) async-start(), calls=%async_computation.1 | async-start | bytes 262144 | tf_op jit(solution)/shard_map/psum | solution.py:27
  7.3 2.1 copy-start.5
  11.2 204.0 %all-reduce.6.cloned.1.call-start = ((), (), s32[]{:S(2)}) async-start(), calls=%async_computation | async-start | bytes 1048576 | tf_op jit(solution)/shard_map/psum | solution.py:35
  19.9 1.3 copy-start.2
  23.5 48.5 %copy-start.8 = (s32[2048]{0:T(1024)S(1)}, s32[2048]{0:T(1024)}, u32[]{:S(2)}) copy-start(s32[2048]{0:T(1024)} %param.17) | copy-start | bytes 24580
  23.5 235.5 %copy-start.13 = (s32[64]{0:T(128)S(1)}, s32[64]{0:T(128)}, u32[]{:S(2)}) copy-start(s32[64]{0:T(128)} %param.15) | copy-start | bytes 772
  71.9 232.4 %all-gather.4.cloned.1.call-start = ((), (), s32[]{:S(2)}) async-start(), calls=%async_computation.2 | async-start | bytes 4456448 | tf_op jit(solution)/shard_map/all_gather | solution.py:41
  256.9 47.5 %copy-start.11 = (f32[64]{0:T(128)}, f32[64]{0:T(128)S(1)}, u32[]{:S(2)}) copy-start(f32[64]{0:T(128)S(1)} %psum.43) | copy-start | bytes 772
  258.8 119.5 %all-reduce.10.cloned.1.call-start = ((), (), s32[]{:S(2)}) async-start(), calls=%async_computation.3 | async-start | bytes 1048576 | tf_op jit(solution)/shard_map/psum | solution.py:45
  309.8 3.2 copy-start.1
  313.0 1.6 copy-start.6
  313.0 1.6 copy-start.9
  314.6 63.7 %copy-start.3 = (f32[2048,64]{0,1:T(8,128)S(1)}, f32[2048,64]{0,1:T(8,128)}, u32[]{:S(2)}) copy-start(f32[2048,64]{0,1:T(8,128)} %all-reduce.6.cloned.1.call-done) | copy-start | bytes 1572868
  314.6 63.7 %copy-start.12 = (f32[64]{0:T(128)S(1)}, f32[64]{0:T(128)}, u32[]{:S(2)}) copy-start(f32[64]{0:T(128)} %copy-done.11) | copy-start | bytes 772
  317.8 113.8 %all-gather.6.cloned.1.call-start = ((), (), s32[]{:S(2)}) async-start(), calls=%async_computation.4 | async-start | bytes 4456448 | tf_op jit(solution)/shard_map/all_gather | solution.py:41
  380.5 124.8 %all-reduce.12.cloned.1.call-start = ((), (), s32[]{:S(2)}) async-start(), calls=%async_computation.5 | async-start | bytes 1048576 | tf_op jit(solution)/shard_map/psum | solution.py:45
  436.9 4.6 copy-start.7
  436.9 4.6 copy-start.10
  441.6 63.7 %copy-start.4 = (f32[2048,64]{0,1:T(8,128)S(1)}, f32[2048,64]{0,1:T(8,128)}, u32[]{:S(2)}) copy-start(f32[2048,64]{0,1:T(8,128)} %get-tuple-element.6) | copy-start | bytes 1572868
  444.8 113.6 %all-gather.8.cloned.1.call-start = ((), (), s32[]{:S(2)}) async-start(), calls=%async_computation.6 | async-start | bytes 4456448 | tf_op jit(solution)/shard_map/all_gather | solution.py:41
  507.1 124.9 %all-reduce.14.cloned.1.call-start = ((), (), s32[]{:S(2)}) async-start(), calls=%async_computation.7 | async-start | bytes 1048576 | tf_op jit(solution)/shard_map/psum | solution.py:45
Sparse Core Ops, SparseCore 0:
  12.1 142.6 all-reduce.7
  157.2 57.9 all-reduce.5
  258.9 45.3 all-gather.3
  317.9 60.3 all-reduce.9
  380.6 50.8 all-gather.5
  444.9 60.3 all-reduce.11
  507.4 50.8 all-gather.7
  571.7 60.3 all-reduce.13
where the time goes:
time: 641 us; the launch traced here: 640 us
  waiting for transfers between devices  471 us (73%)
  other arithmetic  58.8 us (9%)
  blocking collectives  40.5 us (6%)
  local copies, waits for them, and re-layouts  33.6 us (5%)
  matrix products  21.7 us (3%)
  between operations  14.4 us (2%)
    psum x3, waiting for transfers between devices, body(): inflow = lax.psum(gathered.reshape(host_dev, topics), 'doc')  181 us
    all_gather x3, waiting for transfers between devices, body(): full = lax.all_gather(sent, 'hst', axis=0, tiled=True)  147 us
    psum x1, waiting for transfers between devices, body(): degree = lax.psum(degree_blocks, ('hst', 'doc')).reshape(hosts_all)  82.8 us
    psum x1, waiting for transfers between devices, body(): host_topic = lax.psum(local_topic, 'doc')  59.7 us
    scatter-add x1, other arithmetic, body(): local_topic = jax.ops.segment_sum(probs, doc_host, num_segments=host_dev)  44.5 us
    psum x1, blocking collectives, body(): mass = lax.psum(jnp.sum(member[:, None] * host_topic, axis=0), 'hst')  40.5 us
    reshape x3, local copies, waits for them, and re-layouts, body(): slabs = full.reshape(nblocks, block, topics)[src_block]  16.1 us
  transfers between devices with their start and end apart: 8, of which 8 were waited for; matrix products, arithmetic and copies ran while one was open for 9% of the time, Pallas kernels for 0%

commit v1 on v0

--- a/solution.py
+++ b/solution.py
@@ -4,6 +4,27 @@
 from jax.sharding import PartitionSpec as P
 
 HOPS = 3
+
+
+def gather_around(shard, axis, dim):
+    count, position, extent = (lax.axis_size(axis), lax.axis_index(axis), shard.shape[dim])
+    right = [(i, (i + 1) % count) for i in range(count)]
+    downward = [(i, (i - 1) % count) for i in range(count)]
+    whole = jnp.zeros((*shard.shape[:dim], count * extent, *shard.shape[dim + 1 :]), shard.dtype)
+    whole = lax.dynamic_update_slice_in_dim(whole, shard, position * extent, axis=dim)
+    from_left = from_right = shard
+    halfway = count // 2
+    for step in range(1, halfway + 1):
+        from_left = lax.ppermute(from_left, axis, right)
+        whole = lax.dynamic_update_slice_in_dim(
+            whole, from_left, (position - step) % count * extent, axis=dim
+        )
+        if step < count - halfway:
+            from_right = lax.ppermute(from_right, axis, downward)
+            whole = lax.dynamic_update_slice_in_dim(
+                whole, from_right, (position + step) % count * extent, axis=dim
+            )
+    return whole
 
 
 def body(docs, w_in, w_out, doc_host, tiles, dst_block, src_block, tile_count, teleport):
@@ -38,7 +59,7 @@
     state = tele
     for hop in range(HOPS):
         sent = (state * inverse[:, None]).astype(jnp.bfloat16)
-        full = lax.all_gather(sent, "hst", axis=0, tiled=True)
+        full = gather_around(sent, "hst", 0)
         slabs = full.reshape(nblocks, block, topics)[src_block]
         prod = jnp.einsum("kij,kjt->kit", tiles, slabs, preferred_element_type=jnp.float32)
         gathered = jnp.einsum("kb,kit->bit", dst_onehot, prod, precision=lax.Precision.HIGHEST)

time: 641 us -> 729 us (1.14); the launches traced: 640 us -> 720 us
  starting transfers between devices: 0.7 us -> 116 us
  waiting for transfers between devices: 471 us -> 443 us
    all_gather x3 -> x0, waiting for transfers between devices: 147 us -> none  [body(): full = lax.all_gather(sent, 'hst', axis=0, tiled=True)]
    ppermute x0 -> x45, waiting for transfers between devices: none -> 133 us  [the longest x24 132 us: gather_around(): from_left = lax.ppermute(from_left, axis, right)]
    ppermute x0 -> x45, starting transfers between devices: none -> 116 us  [the longest x21 113 us: gather_around(): from_right = lax.ppermute(from_right, axis, downward)]
    psum x3, waiting for transfers between devices: 181 us -> 168 us  [body(): inflow = lax.psum(gathered.reshape(host_dev, topics), 'doc')]
  transfers between devices with their start and end apart: 8 -> 50, of which waited for: 8 -> 31; matrix products, arithmetic and copies ran while one was open for 9% -> 8% of each run, Pallas kernels for 0% -> 0%
where the time goes in v1:
time: 729 us; the launch traced here: 720 us
  waiting for transfers between devices  443 us (61%)
  starting transfers between devices  116 us (16%)
  other arithmetic  53.6 us (7%)
  blocking collectives  40.6 us (6%)
  local copies, waits for them, and re-layouts  30.1 us (4%)
  matrix products  21.7 us (3%)
  between operations  15 us (2%)
    psum x3, waiting for transfers between devices, body(): inflow = lax.psum(gathered.reshape(host_dev, topics), 'doc')  168 us
    ppermute x24, waiting for transfers between devices, gather_around(): from_left = lax.ppermute(from_left, axis, right)  132 us
    ppermute x21, starting transfers between devices, gather_around(): from_right = lax.ppermute(from_right, axis, downward)  113 us
    psum x1, waiting for transfers between devices, body(): degree = lax.psum(degree_blocks, ('hst', 'doc')).reshape(hosts_all)  82.5 us
    psum x1, waiting for transfers between devices, body(): host_topic = lax.psum(local_topic, 'doc')  59.7 us
    scatter-add x1, other arithmetic, body(): local_topic = jax.ops.segment_sum(probs, doc_host, num_segments=host_dev)  44.5 us
    psum x1, blocking collectives, body(): mass = lax.psum(jnp.sum(member[:, None] * host_topic, axis=0), 'hst')  40.6 us
  transfers between devices with their start and end apart: 50, of which 31 were waited for; matrix products, arithmetic and copies ran while one was open for 8% of the time, Pallas kernels for 0%

profile of v1, /device:TPU:0, one launch (start us, length us, event | category | flops | bytes accessed | tf_op | source)
XLA Modules:
  0.0 719.8 jit_solution(14453770393629733993)
XLA Ops:
  11.2 8.6 %fusion.48 = (f32[8192]{0:T(1024)S(1)}, f32[8192,64]{0,1:T(8,128)S(1)}) fusion(bf16[256,64]{0,1:T(8,128)(2,1)} %param.11, bf16[8192,768]{1,0:T(8,128)(2,1)} %param.9, bf16[768,256]{1,0:T(8,128)(2,1)S(1)} %copy-done), kind=kOutput, calls=%fused_computation.126 | convolution fusion | flops 3509051392 | bytes 15138816 | tf_op jit(solution)/shard_map/dot_general | solution.py:40
  26.3 44.5 %scatter_custom_fusion = f32[2048,64]{1,0:T(8,128)S(1)} fusion(s32[8192]{0:T(1024)} %param.12, f32[8192,64]{1,0:T(8,128)} %copy.74, f32[]{:T(128)} %constant.169.clone.1), kind=kCustom, calls=%fused_computation.37 | custom fusion | flops 524288 | bytes 524800 | tf_op jit(solution)/shard_map/scatter-add | solution.py:41
  72.3 82.5 %all-reduce.8.cloned.1.call-done = f32[32768]{0:T(1024)} async-done(((f32[32768]{0:T(1024)}), f32[32768]{0:T(1024)}) %all-reduce.8.cloned.1.call-update) | async-done | bytes 131088 | tf_op jit(solution)/shard_map/psum | solution.py:48
  155.5 59.7 %all-reduce.6.cloned.1.call-done = f32[2048,64]{0,1:T(8,128)} async-done(((f32[2048,64]{0,1:T(8,128)}), f32[2048,64]{0,1:T(8,128)}) %all-reduce.6.cloned.1.call-update) | async-done | bytes 524304 | tf_op jit(solution)/shard_map/psum | solution.py:56
  216.5 40.6 %psum.43 = f32[64]{0:T(128)S(1)} all-reduce(f32[64]{0:T(128)S(1)} %multiply_reduce_fusion), channel_id=1, replica_groups=mesh['hst'=16,'doc'=8] {'hst'}, use_global_device_ids=true, to_apply=%region_5.0 | all-reduce | flops 64 | bytes 512 | tf_op jit(solution)/shard_map/psum | solution.py:57
  263.0 5.7 collective-permute-done
  298.1 5.8 collective-permute-start.9
  307.8 5.9 collective-permute-start.11
  328.2 9.6 %collective-permute-done.14 = bf16[2048,64]{0,1:T(8,128)(2,1)S(1)} collective-permute-done((bf16[2048,64]{0,1:T(8,128)(2,1)S(1)}, bf16[2048,64]{0,1:T(8,128)(2,1)S(1)}, u32[]{:S(2)}, u32[]{:S(2)}) %collective-permute-start.14) | collective-permute-done | bytes 262176 | tf_op jit(solution)/shard_map/ppermute | solution.py:18
  349.0 59.3 %all-reduce.10.cloned.1.call-done = f32[2048,64]{0,1:T(8,128)} async-done(((f32[2048,64]{0,1:T(8,128)}), f32[2048,64]{0,1:T(8,128)}) %all-reduce.10.cloned.1.call-update) | async-done | bytes 524304 | tf_op jit(solution)/shard_map/psum | solution.py:66
  420.1 5.4 collective-permute-start.18
  429.8 5.4 collective-permute-start.20
  439.5 5.4 collective-permute-start.22
  450.0 5.7 collective-permute-start.24
  455.7 5.9 collective-permute-done.23
  461.8 5.8 collective-permute-start.26
  467.6 6.3 collective-permute-done.25
  474.1 5.4 collective-permute-start.28
  479.5 5.9 collective-permute-done.27
  485.5 9.6 %collective-permute-done.29 = bf16[2048,64]{0,1:T(8,128)(2,1)S(1)} collective-permute-done((bf16[2048,64]{0,1:T(8,128)(2,1)S(1)}, bf16[2048,64]{0,1:T(8,128)(2,1)S(1)}, u32[]{:S(2)}, u32[]{:S(2)}) %collective-permute-start.29) | collective-permute-done | bytes 262176 | tf_op jit(solution)/shard_map/ppermute | solution.py:18
  506.1 54.2 %all-reduce.12.cloned.1.call-done = f32[2048,64]{0,1:T(8,128)} async-done(((f32[2048,64]{0,1:T(8,128)}), f32[2048,64]{0,1:T(8,128)}) %all-reduce.12.cloned.1.call-update) | async-done | bytes 524304 | tf_op jit(solution)/shard_map/psum | solution.py:66
  571.3 5.4 collective-permute-start.33
  580.9 5.4 collective-permute-start.35
  590.6 5.4 collective-permute-start.37
  601.1 5.7 collective-permute-start.39
  606.8 5.9 collective-permute-done.38
  613.0 5.8 collective-permute-start.41
  618.8 6.1 collective-permute-done.40
  625.0 5.7 collective-permute-start.43
  630.7 5.8 collective-permute-done.42
  636.8 9.6 %collective-permute-done.44 = bf16[2048,64]{0,1:T(8,128)(2,1)S(1)} collective-permute-done((bf16[2048,64]{0,1:T(8,128)(2,1)S(1)}, bf16[2048,64]{0,1:T(8,128)(2,1)S(1)}, u32[]{:S(2)}, u32[]{:S(2)}) %collective-permute-start.44) | collective-permute-done | bytes 262176 | tf_op jit(solution)/shard_map/ppermute | solution.py:18
  657.3 54.2 %all-reduce.14.cloned.1.call-done = f32[2048,64]{0,1:T(8,128)} async-done(((f32[2048,64]{0,1:T(8,128)}), f32[2048,64]{0,1:T(8,128)}) %all-reduce.14.cloned.1.call-update) | async-done | bytes 524304 | tf_op jit(solution)/shard_map/psum | solution.py:66
  (179 shorter events, 152.5 us)
Async XLA Ops:
  6.5 148.3 %all-reduce.8.cloned.1.call-start = ((), (), s32[]{:S(2)}) async-start(), calls=%async_computation.1 | async-start | bytes 262144 | tf_op jit(solution)/shard_map/psum | solution.py:48
  11.2 204.0 %all-reduce.6.cloned.1.call-start = ((), (), s32[]{:S(2)}) async-start(), calls=%async_computation | async-start | bytes 1048576 | tf_op jit(solution)/shard_map/psum | solution.py:56
  71.9 336.4 %all-reduce.10.cloned.1.call-start = ((), (), s32[]{:S(2)}) async-start(), calls=%async_computation.2 | async-start | bytes 1048576 | tf_op jit(solution)/shard_map/psum | solution.py:66
  257.5 11.1 %collective-permute-start = (bf16[2048,64]{0,1:T(8,128)(2,1)S(1)}, bf16[2048,64]{0,1:T(8,128)(2,1)S(1)}, u32[]{:S(2)}, u32[]{:S(2)}) collective-permute-start(bf16[2048,64]{0,1:T(8,128)(2,1)S(1)} %get-tuple-element.11), channel_id=1, source_target_pairs={{0,8},{8,16},{16,24},{24,32},{32,40},{40,48},{48,56},{56,64},{64,7... | collective-permute-start | bytes 786440 | tf_op jit(solution)/shard_map/ppermute | solution.py:18
  257.6 11.0 %collective-permute-start.1 = (bf16[2048,64]{0,1:T(8,128)(2,1)S(1)}, bf16[2048,64]{0,1:T(8,128)(2,1)S(1)}, u32[]{:S(2)}, u32[]{:S(2)}) collective-permute-start(bf16[2048,64]{0,1:T(8,128)(2,1)S(1)} %get-tuple-element.11), channel_id=1, source_target_pairs={{0,120},{8,0},{16,8},{24,16},{32,24},{40,32},{48,40},{56,48},{64,5... | collective-permute-start | bytes 786440 | tf_op jit(solution)/shard_map/ppermute | solution.py:23
  268.6 10.1 %collective-permute-start.2 = (bf16[2048,64]{0,1:T(8,128)(2,1)S(1)}, bf16[2048,64]{0,1:T(8,128)(2,1)S(1)}, u32[]{:S(2)}, u32[]{:S(2)}) collective-permute-start(bf16[2048,64]{0,1:T(8,128)(2,1)S(1)} %collective-permute-done), channel_id=1, source_target_pairs={{0,8},{8,16},{16,24},{24,32},{32,40},{40,48},{48,56},{56,64},{64,7... | collective-permute-start | bytes 786440 | tf_op jit(solution)/shard_map/ppermute | solution.py:18
  268.6 10.1 %collective-permute-start.3 = (bf16[2048,64]{0,1:T(8,128)(2,1)S(1)}, bf16[2048,64]{0,1:T(8,128)(2,1)S(1)}, u32[]{:S(2)}, u32[]{:S(2)}) collective-permute-start(bf16[2048,64]{0,1:T(8,128)(2,1)S(1)} %collective-permute-done.1), channel_id=1, source_target_pairs={{0,120},{8,0},{16,8},{24,16},{32,24},{40,32},{48,40},{56,48},{64,5... | collective-permute-start | bytes 786440 | tf_op jit(solution)/shard_map/ppermute | solution.py:23
  278.8 9.7 %collective-permute-start.4 = (bf16[2048,64]{0,1:T(8,128)(2,1)S(1)}, bf16[2048,64]{0,1:T(8,128)(2,1)S(1)}, u32[]{:S(2)}, u32[]{:S(2)}) collective-permute-start(bf16[2048,64]{0,1:T(8,128)(2,1)S(1)} %collective-permute-done.2), channel_id=1, source_target_pairs={{0,8},{8,16},{16,24},{24,32},{32,40},{40,48},{48,56},{56,64},{64,7... | collective-permute-start | bytes 786440 | tf_op jit(solution)/shard_map/ppermute | solution.py:18
  298.1 9.7 %collective-permute-start.9 = (bf16[2048,64]{0,1:T(8,128)(2,1)S(1)}, bf16[2048,64]{0,1:T(8,128)(2,1)S(1)}, u32[]{:S(2)}, u32[]{:S(2)}) collective-permute-start(bf16[2048,64]{0,1:T(8,128)(2,1)S(1)} %collective-permute-done.7), channel_id=1, source_target_pairs={{0,120},{8,0},{16,8},{24,16},{32,24},{40,32},{48,40},{56,48},{64,5... | collective-permute-start | bytes 786440 | tf_op jit(solution)/shard_map/ppermute | solution.py:23
  307.8 10.6 %collective-permute-start.10 = (bf16[2048,64]{0,1:T(8,128)(2,1)S(1)}, bf16[2048,64]{0,1:T(8,128)(2,1)S(1)}, u32[]{:S(2)}, u32[]{:S(2)}) collective-permute-start(bf16[2048,64]{0,1:T(8,128)(2,1)S(1)} %collective-permute-done.8), channel_id=1, source_target_pairs={{0,8},{8,16},{16,24},{24,32},{32,40},{40,48},{48,56},{56,64},{64,7... | collective-permute-start | bytes 786440 | tf_op jit(solution)/shard_map/ppermute | solution.py:18
  307.8 10.6 %collective-permute-start.11 = (bf16[2048,64]{0,1:T(8,128)(2,1)S(1)}, bf16[2048,64]{0,1:T(8,128)(2,1)S(1)}, u32[]{:S(2)}, u32[]{:S(2)}) collective-permute-start(bf16[2048,64]{0,1:T(8,128)(2,1)S(1)} %collective-permute-done.9), channel_id=1, source_target_pairs={{0,120},{8,0},{16,8},{24,16},{32,24},{40,32},{48,40},{56,48},{64,5... | collective-permute-start | bytes 786440 | tf_op jit(solution)/shard_map/ppermute | solution.py:23
  318.5 9.7 %collective-permute-start.13 = (bf16[2048,64]{0,1:T(8,128)(2,1)S(1)}, bf16[2048,64]{0,1:T(8,128)(2,1)S(1)}, u32[]{:S(2)}, u32[]{:S(2)}) collective-permute-start(bf16[2048,64]{0,1:T(8,128)(2,1)S(1)} %collective-permute-done.11), channel_id=1, source_target_pairs={{0,120},{8,0},{16,8},{24,16},{32,24},{40,32},{48,40},{56,48},{64,5... | collective-permute-start | bytes 786440 | tf_op jit(solution)/shard_map/ppermute | solution.py:23
  349.0 211.4 %all-reduce.12.cloned.1.call-start = ((), (), s32[]{:S(2)}) async-start(), calls=%async_computation.3 | async-start | bytes 1048576 | tf_op jit(solution)/shard_map/psum | solution.py:66
  439.4 10.5 %collective-permute-start.21 = (bf16[2048,64]{0,1:T(8,128)(2,1)S(1)}, bf16[2048,64]{0,1:T(8,128)(2,1)S(1)}, u32[]{:S(2)}, u32[]{:S(2)}) collective-permute-start(bf16[2048,64]{0,1:T(8,128)(2,1)S(1)} %collective-permute-done.19), channel_id=1, source_target_pairs={{0,8},{8,16},{16,24},{24,32},{32,40},{40,48},{48,56},{56,64},{64,7... | collective-permute-start | bytes 786440 | tf_op jit(solution)/shard_map/ppermute | solution.py:18
  439.5 10.5 %collective-permute-start.22 = (bf16[2048,64]{0,1:T(8,128)(2,1)S(1)}, bf16[2048,64]{0,1:T(8,128)(2,1)S(1)}, u32[]{:S(2)}, u32[]{:S(2)}) collective-permute-start(bf16[2048,64]{0,1:T(8,128)(2,1)S(1)} %collective-permute-done.20), channel_id=1, source_target_pairs={{0,120},{8,0},{16,8},{24,16},{32,24},{40,32},{48,40},{56,48},{64,5... | collective-permute-start | bytes 786440 | tf_op jit(solution)/shard_map/ppermute | solution.py:23
  449.9 11.7 %collective-permute-start.23 = (bf16[2048,64]{0,1:T(8,128)(2,1)S(1)}, bf16[2048,64]{0,1:T(8,128)(2,1)S(1)}, u32[]{:S(2)}, u32[]{:S(2)}) collective-permute-start(bf16[2048,64]{0,1:T(8,128)(2,1)S(1)} %collective-permute-done.21), channel_id=1, source_target_pairs={{0,8},{8,16},{16,24},{24,32},{32,40},{40,48},{48,56},{56,64},{64,7... | collective-permute-start | bytes 786440 | tf_op jit(solution)/shard_map/ppermute | solution.py:18
  450.0 11.9 %collective-permute-start.24 = (bf16[2048,64]{0,1:T(8,128)(2,1)S(1)}, bf16[2048,64]{0,1:T(8,128)(2,1)S(1)}, u32[]{:S(2)}, u32[]{:S(2)}) collective-permute-start(bf16[2048,64]{0,1:T(8,128)(2,1)S(1)} %collective-permute-done.22), channel_id=1, source_target_pairs={{0,120},{8,0},{16,8},{24,16},{32,24},{40,32},{48,40},{56,48},{64,5... | collective-permute-start | bytes 786440 | tf_op jit(solution)/shard_map/ppermute | solution.py:23
  461.6 12.4 %collective-permute-start.25 = (bf16[2048,64]{0,1:T(8,128)(2,1)S(1)}, bf16[2048,64]{0,1:T(8,128)(2,1)S(1)}, u32[]{:S(2)}, u32[]{:S(2)}) collective-permute-start(bf16[2048,64]{0,1:T(8,128)(2,1)S(1)} %collective-permute-done.23), channel_id=1, source_target_pairs={{0,8},{8,16},{16,24},{24,32},{32,40},{40,48},{48,56},{56,64},{64,7... | collective-permute-start | bytes 786440 | tf_op jit(solution)/shard_map/ppermute | solution.py:18
  461.8 12.3 %collective-permute-start.26 = (bf16[2048,64]{0,1:T(8,128)(2,1)S(1)}, bf16[2048,64]{0,1:T(8,128)(2,1)S(1)}, u32[]{:S(2)}, u32[]{:S(2)}) collective-permute-start(bf16[2048,64]{0,1:T(8,128)(2,1)S(1)} %collective-permute-done.24), channel_id=1, source_target_pairs={{0,120},{8,0},{16,8},{24,16},{32,24},{40,32},{48,40},{56,48},{64,5... | collective-permute-start | bytes 786440 | tf_op jit(solution)/shard_map/ppermute | solution.py:23
  473.9 11.5 %collective-permute-start.27 = (bf16[2048,64]{0,1:T(8,128)(2,1)S(1)}, bf16[2048,64]{0,1:T(8,128)(2,1)S(1)}, u32[]{:S(2)}, u32[]{:S(2)}) collective-permute-start(bf16[2048,64]{0,1:T(8,128)(2,1)S(1)} %collective-permute-done.25), channel_id=1, source_target_pairs={{0,8},{8,16},{16,24},{24,32},{32,40},{40,48},{48,56},{56,64},{64,7... | collective-permute-start | bytes 786440 | tf_op jit(solution)/shard_map/ppermute | solution.py:18
  474.1 11.3 %collective-permute-start.28 = (bf16[2048,64]{0,1:T(8,128)(2,1)S(1)}, bf16[2048,64]{0,1:T(8,128)(2,1)S(1)}, u32[]{:S(2)}, u32[]{:S(2)}) collective-permute-start(bf16[2048,64]{0,1:T(8,128)(2,1)S(1)} %collective-permute-done.26), channel_id=1, source_target_pairs={{0,120},{8,0},{16,8},{24,16},{32,24},{40,32},{48,40},{56,48},{64,5... | collective-permute-start | bytes 786440 | tf_op jit(solution)/shard_map/ppermute | solution.py:23
  506.0 205.5 %all-reduce.14.cloned.1.call-start = ((), (), s32[]{:S(2)}) async-start(), calls=%async_computation.4 | async-start | bytes 1048576 | tf_op jit(solution)/shard_map/psum | solution.py:66
  561.5 9.8 %collective-permute-start.30 = (bf16[2048,64]{0,1:T(8,128)(2,1)S(1)}, bf16[2048,64]{0,1:T(8,128)(2,1)S(1)}, u32[]{:S(2)}, u32[]{:S(2)}) collective-permute-start(bf16[2048,64]{0,1:T(8,128)(2,1)S(1)} %get-tuple-element.6), channel_id=1, source_target_pairs={{0,8},{8,16},{16,24},{24,32},{32,40},{40,48},{48,56},{56,64},{64,7... | collective-permute-start | bytes 786440 | tf_op jit(solution)/shard_map/ppermute | solution.py:18
  590.6 10.5 %collective-permute-start.36 = (bf16[2048,64]{0,1:T(8,128)(2,1)S(1)}, bf16[2048,64]{0,1:T(8,128)(2,1)S(1)}, u32[]{:S(2)}, u32[]{:S(2)}) collective-permute-start(bf16[2048,64]{0,1:T(8,128)(2,1)S(1)} %collective-permute-done.34), channel_id=1, source_target_pairs={{0,8},{8,16},{16,24},{24,32},{32,40},{40,48},{48,56},{56,64},{64,7... | collective-permute-start | bytes 786440 | tf_op jit(solution)/shard_map/ppermute | solution.py:18
  590.6 10.5 %collective-permute-start.37 = (bf16[2048,64]{0,1:T(8,128)(2,1)S(1)}, bf16[2048,64]{0,1:T(8,128)(2,1)S(1)}, u32[]{:S(2)}, u32[]{:S(2)}) collective-permute-start(bf16[2048,64]{0,1:T(8,128)(2,1)S(1)} %collective-permute-done.35), channel_id=1, source_target_pairs={{0,120},{8,0},{16,8},{24,16},{32,24},{40,32},{48,40},{56,48},{64,5... | collective-permute-start | bytes 786440 | tf_op jit(solution)/shard_map/ppermute | solution.py:23
  601.1 11.7 %collective-permute-start.38 = (bf16[2048,64]{0,1:T(8,128)(2,1)S(1)}, bf16[2048,64]{0,1:T(8,128)(2,1)S(1)}, u32[]{:S(2)}, u32[]{:S(2)}) collective-permute-start(bf16[2048,64]{0,1:T(8,128)(2,1)S(1)} %collective-permute-done.36), channel_id=1, source_target_pairs={{0,8},{8,16},{16,24},{24,32},{32,40},{40,48},{48,56},{56,64},{64,7... | collective-permute-start | bytes 786440 | tf_op jit(solution)/shard_map/ppermute | solution.py:18
  601.1 11.9 %collective-permute-start.39 = (bf16[2048,64]{0,1:T(8,128)(2,1)S(1)}, bf16[2048,64]{0,1:T(8,128)(2,1)S(1)}, u32[]{:S(2)}, u32[]{:S(2)}) collective-permute-start(bf16[2048,64]{0,1:T(8,128)(2,1)S(1)} %collective-permute-done.37), channel_id=1, source_target_pairs={{0,120},{8,0},{16,8},{24,16},{32,24},{40,32},{48,40},{56,48},{64,5... | collective-permute-start | bytes 786440 | tf_op jit(solution)/shard_map/ppermute | solution.py:23
  612.7 12.2 %collective-permute-start.40 = (bf16[2048,64]{0,1:T(8,128)(2,1)S(1)}, bf16[2048,64]{0,1:T(8,128)(2,1)S(1)}, u32[]{:S(2)}, u32[]{:S(2)}) collective-permute-start(bf16[2048,64]{0,1:T(8,128)(2,1)S(1)} %collective-permute-done.38), channel_id=1, source_target_pairs={{0,8},{8,16},{16,24},{24,32},{32,40},{40,48},{48,56},{56,64},{64,7... | collective-permute-start | bytes 786440 | tf_op jit(solution)/shard_map/ppermute | solution.py:18
  613.0 12.0 %collective-permute-start.41 = (bf16[2048,64]{0,1:T(8,128)(2,1)S(1)}, bf16[2048,64]{0,1:T(8,128)(2,1)S(1)}, u32[]{:S(2)}, u32[]{:S(2)}) collective-permute-start(bf16[2048,64]{0,1:T(8,128)(2,1)S(1)} %collective-permute-done.39), channel_id=1, source_target_pairs={{0,120},{8,0},{16,8},{24,16},{32,24},{40,32},{48,40},{56,48},{64,5... | collective-permute-start | bytes 786440 | tf_op jit(solution)/shard_map/ppermute | solution.py:23
  624.9 11.5 %collective-permute-start.42 = (bf16[2048,64]{0,1:T(8,128)(2,1)S(1)}, bf16[2048,64]{0,1:T(8,128)(2,1)S(1)}, u32[]{:S(2)}, u32[]{:S(2)}) collective-permute-start(bf16[2048,64]{0,1:T(8,128)(2,1)S(1)} %collective-permute-done.40), channel_id=1, source_target_pairs={{0,8},{8,16},{16,24},{24,32},{32,40},{40,48},{48,56},{56,64},{64,7... | collective-permute-start | bytes 786440 | tf_op jit(solution)/shard_map/ppermute | solution.py:18
  625.0 11.7 %collective-permute-start.43 = (bf16[2048,64]{0,1:T(8,128)(2,1)S(1)}, bf16[2048,64]{0,1:T(8,128)(2,1)S(1)}, u32[]{:S(2)}, u32[]{:S(2)}) collective-permute-start(bf16[2048,64]{0,1:T(8,128)(2,1)S(1)} %collective-permute-done.41), channel_id=1, source_target_pairs={{0,120},{8,0},{16,8},{24,16},{32,24},{40,32},{48,40},{56,48},{64,5... | collective-permute-start | bytes 786440 | tf_op jit(solution)/shard_map/ppermute | solution.py:23
  636.5 9.9 %collective-permute-start.44 = (bf16[2048,64]{0,1:T(8,128)(2,1)S(1)}, bf16[2048,64]{0,1:T(8,128)(2,1)S(1)}, u32[]{:S(2)}, u32[]{:S(2)}) collective-permute-start(bf16[2048,64]{0,1:T(8,128)(2,1)S(1)} %collective-permute-done.42), channel_id=1, source_target_pairs={{0,8},{8,16},{16,24},{24,32},{32,40},{40,48},{48,56},{56,64},{64,7... | collective-permute-start | bytes 786440 | tf_op jit(solution)/shard_map/ppermute | solution.py:18
  (30 other events, 654.7 us)
Sparse Core Ops, SparseCore 0:
  12.1 142.6 all-reduce.7
  157.2 57.9 all-reduce.5
  349.1 59.2 all-reduce.9
  506.2 54.1 all-reduce.11
  657.5 54.0 all-reduce.13
